TPU v7x, 32 devices: a whole 2x2x4 slice. The times are simulated.
32 devices in a mesh: dp: 8 (over z, x), expert: 4 (over y, core).
Axes of the slice: x: 2, y: 2, z: 4, core: 2. Of those that a mesh axis runs over, the one named last changes fastest.
Arguments:
- grad_output: bfloat16 [512, 6144], P('expert', 'dp'), may hold values from -6 to 6
- gate_probs: float32 [512, 4], P('expert'), may hold values from 0.05 to 1
- routing: int32 [512, 4], P('expert'), may hold values from 0 to 15, all different within a row; in each aligned block of 128 rows (0 to 127, 128 to 255, ...) at most 40 rows name the same one
- old_weights: bfloat16 [16, 1024, 6144], P('expert', None, 'dp'), may hold values from -0.1875 to 0.1875
- old_slot_expert: int32 [16], replicated, may hold values from 0 to 15, each once
- new_slot_expert: int32 [16], replicated, may hold values from 0 to 15, each once
- saved_hidden: bfloat16 [16, 160, 1024], P('expert'), may hold values from -6 to 6
- shared_hidden: bfloat16 [512, 1024], P('expert'), may hold values from -6 to 6
- shared_weight: bfloat16 [1024, 6144], P('expert', 'dp'), may hold values from -0.1875 to 0.1875
Outputs:
- expert_weight_grad: bfloat16 [16, 1024, 6144], P('expert', None, 'dp')
- expert_hidden_grad: bfloat16 [16, 160, 1024], P('expert', 'dp')
- shared_hidden_grad: bfloat16 [512, 1024], P('expert', 'dp')
- shared_weight_grad: bfloat16 [1024, 6144], P('expert', 'dp')
Inputs may be any that keep to these rules, and one draw needn't show every extreme that they name: `routing`: each row names 4 different experts. Among the 128 rows of one group no expert is named by more than 40 rows, a bound that some block reaches of them. `old_slot_expert`: A permutation of the experts. `new_slot_expert`: A permutation of the experts.
All inputs are finite; a program needn't handle non-finite values.
Results may differ from a plain program's by a relative error of at most 0.023.
Values may be sent and summed in bfloat16 or wider, within the bound.
A program may use at most 64 MiB of HBM per device.

v0:
```python
import functools

import jax
import jax.numpy as jnp
from jax import lax
from jax.experimental import pallas as pl
from jax.experimental.pallas import tpu as pltpu
from jax.sharding import PartitionSpec as P

MESH = pl.DeviceIdType.MESH
F32 = jnp.float32
BF16 = jnp.bfloat16
CHUNKS = 4


def remote(src, dst, send, recv, device):
    return pltpu.make_async_remote_copy(
        src_ref=src, dst_ref=dst, send_sem=send, recv_sem=recv, device_id=device, device_id_type=MESH
    )


def exchange_kernel(
    n_dp,
    n_ex,
    sliced,
    grad_ref,
    route_ref,
    gate_ref,
    old_hbm,
    new_hbm,
    hidden_ref,
    shared_ref,
    weights_hbm,
    saved_hbm,
    expert_grad_hbm,
    routed_ref,
    hidden_grad_ref,
    weight_grad_ref,
    old_ref,
    new_ref,
    weights,
    saved,
    expert_grad,
    rows,
    grads,
    routes,
    gate_tables,
    hiddens,
    shareds,
    picked,
    product,
    stage,
    part,
    part_in,
    pair_sum,
    ring_in,
    total,
    gathered,
    spart,
    spart_in,
    spair_sum,
    sring_in,
    local_sem,
    own_sem,
    out_sem,
    route_sem,
    gate_sem,
    grad_sem,
    grad_pair_sem,
    shared_sem,
    shared_pair_sem,
    hidden_sem,
    pair_sem,
    ring_sem,
    spread_sem,
):
    d, g = lax.axis_index("dp"), lax.axis_index("expert")
    n_z, n_y = n_dp // 2, n_ex // 2
    z, x = d // 2, lax.rem(d, 2)
    y, c = g // 2, lax.rem(g, 2)
    local, slot_rows, columns = rows.shape
    cap = slot_rows // n_ex
    tok = grad_ref.shape[0]
    tokens = tok * n_ex
    chosen = route_ref.shape[0]
    piece = slot_rows // n_dp
    hidden = weights.shape[1]
    width = hidden // CHUNKS

    def pair_of(first):
        return (d, first * 2 + (1 - c))

    def line_dest(dy):
        return lax.rem(y + dy, n_y) * 2 + c

    def line_source(dy):
        return lax.rem(y + n_y - dy, n_y) * 2 + c

    unit = hiddens.shape[2]

    def hidden_piece(owner):
        if sliced:
            return hidden_ref.at[:, pl.ds(pl.multiple_of(owner * unit, unit), unit)]
        return hidden_ref.at[owner]

    own = [
        (old_hbm, old_ref),
        (new_hbm, new_ref),
        (route_ref, routes.at[g]),
        (gate_ref, gate_tables.at[g]),
        (grad_ref, grads.at[g]),
        (shared_ref, shareds.at[g]),
        (hidden_piece(g), hiddens.at[g]),
        (saved_hbm, saved),
    ]
    own = [pltpu.make_async_copy(a, b, own_sem.at[i]) for i, (a, b) in enumerate(own)]
    for copy in own:
        copy.start()
    loads = []
    for k in range(CHUNKS):
        cut = pl.ds(k * width, width)
        loads.append(
            pltpu.make_async_copy(weights_hbm.at[:, cut], weights.at[:, cut], local_sem.at[k])
        )
        loads[-1].start()

    barrier = pltpu.get_barrier_semaphore()
    peers = [(d, lax.rem(g + k, n_ex)) for k in range(1, n_ex)]
    peers += [(z * 2 + (1 - x), g)]
    peers += [(lax.rem(z + k, n_z) * 2 + x, g) for k in range(1, n_z)]
    for peer in peers:
        pl.semaphore_signal(barrier, inc=1, device_id=peer, device_id_type=MESH)
    pl.semaphore_wait(barrier, len(peers))

    sent = []

    def send(copy):
        copy.start()
        sent.append(copy)

    def gather_start(ref, buffer, sem, pair):
        for k in range(1, n_y):
            send(remote(ref, buffer.at[g], sem.at[0, k], sem.at[1, k], (d, line_dest(k))))
        send(remote(ref, buffer.at[g], pair.at[0, 0], pair.at[1, 0], (d, y * 2 + (1 - c))))

    def gather_forward(ref, buffer, sem, pair):
        for k in range(1, n_y):
            source = line_source(k)
            remote(ref, buffer.at[source], sem.at[0, k], sem.at[1, k], (d, source)).wait_recv()
            block = buffer.at[source]
            send(remote(block, block, pair.at[0, k], pair.at[1, k], (d, y * 2 + (1 - c))))

    def gather_end(ref, buffer, sem, pair):
        for k in range(n_y):
            source = lax.rem(y + n_y - k, n_y) * 2 + (1 - c)
            remote(ref, buffer.at[source], pair.at[0, k], pair.at[1, k], (d, source)).wait_recv()

    for k in range(1, n_ex):
        peer = lax.rem(g + k, n_ex)
        send(remote(route_ref, routes.at[g], route_sem.at[0, k], route_sem.at[1, k], (d, peer)))
        send(remote(gate_ref, gate_tables.at[g], gate_sem.at[0, k], gate_sem.at[1, k], (d, peer)))
    gather_start(grad_ref, grads, grad_sem, grad_pair_sem)

    for k in range(1, n_ex):
        source = lax.rem(g + n_ex - k, n_ex)
        remote(
            route_ref, routes.at[source], route_sem.at[0, k], route_sem.at[1, k], (d, source)
        ).wait_recv()
        remote(
            gate_ref, gate_tables.at[source], gate_sem.at[0, k], gate_sem.at[1, k], (d, source)
        ).wait_recv()
    for copy in own[:4]:
        copy.wait()
    place = lax.broadcasted_iota(jnp.int32, (2 * local, 1), 0)
    labels = jnp.zeros((2 * local, 1), F32)
    for s in range(local):
        labels = jnp.where(place == s, old_ref[g * local + s].astype(F32), labels)
        labels = jnp.where(place == local + s, new_ref[g * local + s].astype(F32), labels)
    before = (
        lax.broadcasted_iota(jnp.int32, (tok, tok), 0)
        < lax.broadcasted_iota(jnp.int32, (tok, tok), 1)
    ).astype(BF16)
    codes, gates = [], []
    for p in range(n_ex):
        table, gate_table = routes[p].astype(F32), gate_tables[p]
        named = jnp.zeros((2 * local, tok), F32)
        gate = jnp.zeros((2 * local, tok), F32)
        for k in range(chosen):
            hit = table[k : k + 1, :] == labels
            named = jnp.where(hit, 1.0, named)
            gate = jnp.where(hit, gate_table[k : k + 1, :], gate)
        rank = jnp.dot(named.astype(BF16), before, preferred_element_type=F32)
        codes.append(jnp.where(named > 0, rank + float(p * cap), -1.0))
        gates.append(gate)
    code = jnp.concatenate(codes, axis=1)
    gate = jnp.concatenate(gates, axis=1)
    row = lax.broadcasted_iota(jnp.int32, (slot_rows, tokens), 0).astype(F32)

    def build(s, tokens_in):
        hit = code[s : s + 1, :] == row
        scale = jnp.sum(jnp.where(hit, gate[s : s + 1, :], 0.0), axis=1, keepdims=True)
        chosen_rows = jnp.dot(hit.astype(BF16), tokens_in, preferred_element_type=F32)
        return (chosen_rows * scale).astype(BF16)

    gather_forward(grad_ref, grads, grad_sem, grad_pair_sem)
    gather_start(shared_ref, shareds, shared_sem, shared_pair_sem)
    for k in range(1, n_ex):
        peer = lax.rem(g + k, n_ex)
        send(
            remote(
                hidden_piece(peer), hiddens.at[g], hidden_sem.at[0, k], hidden_sem.at[1, k], (d, peer)
            )
        )
    gather_end(grad_ref, grads, grad_sem, grad_pair_sem)
    own[4].wait()
    all_tokens = grads[...].reshape(tokens, columns)

    for s in range(local):
        picked[s] = build(s, all_tokens)

    def pair_send(k, source, target):
        send(
            remote(
                source.at[1 - x], target, pair_sem.at[0, k], pair_sem.at[1, k], (z * 2 + (1 - x), g)
            )
        )

    for k in range(CHUNKS):
        loads[k].wait()
        for s in range(local):
            product[...] = lax.dot_general(
                picked[s],
                weights[s, k * width : (k + 1) * width, :],
                (((1,), (1,)), ((), ())),
                preferred_element_type=F32,
            )
            for t in range(n_dp):
                stage[t, s * piece : (s + 1) * piece, :] = product[t * piece : (t + 1) * piece, :]
        for t in range(n_dp):
            part[k, t % 2, t // 2] = stage[t].astype(BF16)
        pair_send(k, part.at[k], part_in.at[k])

    gather_forward(shared_ref, shareds, shared_sem, shared_pair_sem)
    for s in range(local):
        rows[s] = build(local + s, all_tokens)
    gather_end(shared_ref, shareds, shared_sem, shared_pair_sem)
    own[5].wait()
    units = shared_ref.shape[0] * n_ex
    shared_all = shareds[...].reshape(units, columns)
    share = units // n_dp
    own_tokens = grads[g]
    for t in range(n_dp):
        spart[t % 2, t // 2] = lax.dot_general(
            own_tokens,
            shared_all[t * share : (t + 1) * share, :],
            (((1,), (1,)), ((), ())),
            preferred_element_type=F32,
        ).astype(BF16)
    pair_send(CHUNKS, spart, spart_in)

    def ring_start(k, own, arrived, sums, landing):
        remote(
            own.at[x], arrived, pair_sem.at[0, k], pair_sem.at[1, k], (z * 2 + (1 - x), g)
        ).wait_recv()
        sums[...] = (own[x].astype(F32) + arrived[...].astype(F32)).astype(BF16)
        for step in range(1, n_z):
            to = lax.rem(z + step, n_z)
            send(
                remote(
                    sums.at[to],
                    landing.at[step - 1],
                    ring_sem.at[0, k, step],
                    ring_sem.at[1, k, step],
                    (to * 2 + x, g),
                )
            )

    def ring_end(k, sums, landing):
        result = sums[z].astype(F32)
        for step in range(1, n_z):
            source = lax.rem(z + n_z - step, n_z)
            remote(
                sums.at[z],
                landing.at[step - 1],
                ring_sem.at[0, k, step],
                ring_sem.at[1, k, step],
                (source * 2 + x, g),
            ).wait_recv()
            result = result + landing[step - 1].astype(F32)
        return result.astype(BF16)

    own[6].wait()
    own[7].wait()
    stores = []

    def expert_weight_grad(s):
        expert_grad[s] = lax.dot_general(
            saved[s], rows[s], (((0,), (0,)), ((), ())), preferred_element_type=F32
        ).astype(BF16)
        stores.append(pltpu.make_async_copy(expert_grad.at[s], expert_grad_hbm.at[s], out_sem.at[s]))
        stores[-1].start()

    for k in range(CHUNKS):
        if k < local:
            expert_weight_grad(k)
        ring_start(k, part.at[k], part_in.at[k], pair_sum.at[k], ring_in.at[k])
        if k == 1:
            for j in range(1, n_ex):
                source = lax.rem(g + n_ex - j, n_ex)
                remote(
                    hidden_piece(source),
                    hiddens.at[source],
                    hidden_sem.at[0, j],
                    hidden_sem.at[1, j],
                    (d, source),
                ).wait_recv()
            weight_grad_ref[...] = lax.dot_general(
                hiddens[...].reshape(tokens, unit),
                all_tokens,
                (((0,), (0,)), ((), ())),
                preferred_element_type=F32,
            ).astype(BF16)
    for s in range(CHUNKS, local):
        expert_weight_grad(s)
    ring_start(CHUNKS, spart, spart_in, spair_sum, sring_in)

    for k in range(CHUNKS):
        total[k] = ring_end(k, pair_sum.at[k], ring_in.at[k])
        gathered[k, g] = total[k]
        for j in range(1, n_ex):
            send(
                remote(
                    total.at[k],
                    gathered.at[k, g],
                    spread_sem.at[0, k, j],
                    spread_sem.at[1, k, j],
                    (d, lax.rem(g + j, n_ex)),
                )
            )
    hidden_grad_ref[...] = ring_end(CHUNKS, spair_sum, sring_in)

    high = lax.broadcasted_iota(jnp.int32, (piece, local * piece), 0)
    wide = lax.broadcasted_iota(jnp.int32, (piece, local * piece), 1)
    for k in range(CHUNKS):
        for j in range(1, n_ex):
            source = lax.rem(g + n_ex - j, n_ex)
            remote(
                total.at[k],
                gathered.at[k, source],
                spread_sem.at[0, k, j],
                spread_sem.at[1, k, j],
                (d, source),
            ).wait_recv()
        for s in range(local):
            wanted = new_ref[g * local + s]
            found = jnp.zeros((piece, width), F32)
            for p in range(n_ex):
                choice = jnp.zeros((piece, local * piece), F32)
                for q in range(local):
                    same = jnp.where(old_ref[p * local + q] == wanted, 1.0, 0.0)
                    choice = jnp.where(wide == high + q * piece, same, choice)
                found = found + jnp.dot(
                    choice.astype(BF16), gathered[k, p], preferred_element_type=F32
                )
            routed_ref[s, :, k * width : (k + 1) * width] = found.astype(BF16)

    for copy in stores:
        copy.wait()
    for copy in sent:
        copy.wait_send()


def on_device(
    n_dp,
    n_ex,
    grad_output,
    gate_probs,
    routing,
    old_weights,
    old_slot_expert,
    new_slot_expert,
    saved_hidden,
    shared_hidden,
    shared_weight,
):
    local, hidden, columns = old_weights.shape
    slot_rows = saved_hidden.shape[1]
    tok, chosen = routing.shape
    units_here = shared_weight.shape[0]
    units = shared_hidden.shape[1]
    sliced = units_here % 128 == 0
    if not sliced:
        shared_hidden = shared_hidden.reshape(tok, n_ex, units_here).transpose(1, 0, 2)
    piece = slot_rows // n_dp
    packed = local * piece
    width = hidden // CHUNKS
    share = units // n_dp
    n_z, n_y = n_dp // 2, n_ex // 2
    vmem = pl.BlockSpec(memory_space=pltpu.VMEM)
    anywhere = pl.BlockSpec(memory_space=pl.ANY)
    sem = pltpu.SemaphoreType.DMA
    expert_weight_grad, routed, hidden_grad, weight_grad = pl.pallas_call(
        functools.partial(exchange_kernel, n_dp, n_ex, sliced),
        out_shape=(
            jax.ShapeDtypeStruct((local, hidden, columns), BF16),
            jax.ShapeDtypeStruct((local, piece, hidden), BF16),
            jax.ShapeDtypeStruct((tok, share), BF16),
            jax.ShapeDtypeStruct((units_here, columns), BF16),
        ),
        in_specs=[anywhere] * 9,
        out_specs=(anywhere, vmem, vmem, vmem),
        scratch_shapes=[
            pltpu.SMEM(old_slot_expert.shape, jnp.int32),
            pltpu.SMEM(new_slot_expert.shape, jnp.int32),
            pltpu.VMEM((local, hidden, columns), BF16),
            pltpu.VMEM(saved_hidden.shape, BF16),
            pltpu.VMEM((local, hidden, columns), BF16),
            pltpu.VMEM((local, slot_rows, columns), BF16),
            pltpu.VMEM((n_ex, tok, columns), BF16),
            pltpu.VMEM((n_ex, chosen, tok), jnp.int32),
            pltpu.VMEM((n_ex, chosen, tok), F32),
            pltpu.VMEM((n_ex, tok, units_here), BF16),
            pltpu.VMEM((n_ex, units_here, columns), BF16),
            pltpu.VMEM((local, slot_rows, columns), BF16),
            pltpu.VMEM((slot_rows, width), F32),
            pltpu.VMEM((n_dp, packed, width), F32),
            pltpu.VMEM((CHUNKS, 2, n_z, packed, width), BF16),
            pltpu.VMEM((CHUNKS, n_z, packed, width), BF16),
            pltpu.VMEM((CHUNKS, n_z, packed, width), BF16),
            pltpu.VMEM((CHUNKS, n_z - 1, packed, width), BF16),
            pltpu.VMEM((CHUNKS, packed, width), BF16),
            pltpu.VMEM((CHUNKS, n_ex, packed, width), BF16),
            pltpu.VMEM((2, n_z, tok, share), BF16),
            pltpu.VMEM((n_z, tok, share), BF16),
            pltpu.VMEM((n_z, tok, share), BF16),
            pltpu.VMEM((n_z - 1, tok, share), BF16),
            sem((CHUNKS,)),
            sem((8,)),
            sem((local,)),
            sem((2, n_ex)),
            sem((2, n_ex)),
            sem((2, n_y)),
            sem((2, n_y)),
            sem((2, n_y)),
            sem((2, n_y)),
            sem((2, n_ex)),
            sem((2, CHUNKS + 1)),
            sem((2, CHUNKS + 1, n_z)),
            sem((2, CHUNKS, n_ex)),
        ],
        compiler_params=pltpu.CompilerParams(
            collective_id=0, has_side_effects=True, vmem_limit_bytes=60 * 1024 * 1024
        ),
    )(
        grad_output,
        routing.T,
        gate_probs.T,
        old_slot_expert,
        new_slot_expert,
        shared_hidden,
        shared_weight,
        old_weights,
        saved_hidden,
    )
    return expert_weight_grad, routed, hidden_grad, weight_grad


def solution(mesh):
    return jax.shard_map(
        functools.partial(on_device, mesh.shape["dp"], mesh.shape["expert"]),
        mesh=mesh,
        in_specs=(
            P("expert", "dp"),
            P("expert", None),
            P("expert", None),
            P("expert", None, "dp"),
            P(),
            P(),
            P("expert", None, None),
            P("expert", None),
            P("expert", "dp"),
        ),
        out_specs=(
            P("expert", None, "dp"),
            P("expert", "dp", None),
            P("expert", "dp"),
            P("expert", "dp"),
        ),
        check_vma=False,
    )
```

profile of v0, /device:TPU:0, one launch (start us, length us, event | category | flops | bytes accessed | tf_op | source)
XLA Modules:
  0.0 56.6 jit_solution(9597818959404183172)
XLA Ops:
  0.6 47.0 %shard_map.120 = (bf16[4,1024,768]{2,1,0:T(8,128)(2,1)}, bf16[4,20,1024]{2,1,0:T(8,128)(2,1)}, bf16[128,128]{1,0:T(8,128)(2,1)}, bf16[256,768]{1,0:T(8,128)(2,1)}) custom-call(bf16[128,768]{1,0:T(8,128)(2,1)} %grad_ref.1, s32[4,128]{1,0:T(4,128)} %bitcast.2, f32[4,128]{1,0:T(4,128)} %bitcast.3, s32[16]{0:T(128)} %old_hbm.1, s32[16]{0:T(128)} %new_hbm.1, ...), custom_call_target="tpu_custom_call" | custom-call | tf_op jit(solution)/shard_map/pallas_call | solution.py:402
  47.6 1.7 %copy.13 = bf16[4,20,1024]{2,0,1:T(4,128)(2,1)} copy(bf16[4,20,1024]{2,1,0:T(8,128)(2,1)} %get-tuple-element.5) | data formatting | bytes 327680 | tf_op jit(solution)/shard_map/pallas_call | solution.py:402
  49.3 0.0 copy-start.1
  49.3 0.0 copy-start
  49.3 5.9 %copy.17 = bf16[4,1024,768]{2,1,0:T(8,128)(2,1)} copy(bf16[4,1024,768]{2,1,0:T(8,128)(2,1)} %get-tuple-element.12) | data formatting | bytes 12582912
  55.3 0.0 copy-done.1
  55.3 0.6 %copy.18 = bf16[128,128]{1,0:T(8,128)(2,1)} copy(bf16[128,128]{1,0:T(8,128)(2,1)S(1)} %copy-done.1) | data formatting | bytes 65536
  55.9 0.0 copy-done
  55.9 0.7 %copy.19 = bf16[256,768]{1,0:T(8,128)(2,1)} copy(bf16[256,768]{1,0:T(8,128)(2,1)S(1)} %copy-done) | data formatting | bytes 786432
Async XLA Ops:
  49.3 5.9 %copy-start.1 = (bf16[128,128]{1,0:T(8,128)(2,1)S(1)}, bf16[128,128]{1,0:T(8,128)(2,1)}, u32[]{:S(2)}) copy-start(bf16[128,128]{1,0:T(8,128)(2,1)} %get-tuple-element.14) | copy-start | bytes 98308
  49.3 6.6 %copy-start = (bf16[256,768]{1,0:T(8,128)(2,1)S(1)}, bf16[256,768]{1,0:T(8,128)(2,1)}, u32[]{:S(2)}) copy-start(bf16[256,768]{1,0:T(8,128)(2,1)} %get-tuple-element.15) | copy-start | bytes 1179652
where the time goes:
time: 56.8 us; the launch traced here: 56.6 us
  Pallas kernels  47 us (83%)
  local copies, waits for them, and re-layouts  9.03 us (16%)
  between operations  0.65 us (1%)
    pallas_call x1, Pallas kernels, on_device(): pl.pallas_call(functools.partial(exchange_kernel, n_dp, n_ex, sliced), ou...  47 us
    unnamed x7, local copies, waits for them, and re-layouts  7.31 us
    pallas_call x1, local copies, waits for them, and re-layouts, on_device(): pl.pallas_call(functools.partial(exchange_kernel, n_dp, n_ex, sliced), ou...  1.72 us

commit v1 on v0

--- a/solution.py
+++ b/solution.py
@@ -10,7 +10,7 @@
 MESH = pl.DeviceIdType.MESH
 F32 = jnp.float32
 BF16 = jnp.bfloat16
-CHUNKS = 4
+CHUNKS = 2
 
 
 def remote(src, dst, send, recv, device):
@@ -53,7 +53,9 @@
     part,
     part_in,
     pair_sum,
-    ring_in,
+    near_in,
+    near_sum,
+    far_in,
     total,
     gathered,
     spart,
@@ -71,6 +73,8 @@
     shared_pair_sem,
     hidden_sem,
     pair_sem,
+    near_sem,
+    far_sem,
     ring_sem,
     spread_sem,
 ):
@@ -84,6 +88,9 @@
     tokens = tok * n_ex
     chosen = route_ref.shape[0]
     piece = slot_rows // n_dp
+    near, steps = part.shape[2], part.shape[3]
+    part_rows = slot_rows // n_y
+    units_sent = n_y * CHUNKS
     hidden = weights.shape[1]
     width = hidden // CHUNKS
 
@@ -150,8 +157,8 @@
             block = buffer.at[source]
             send(remote(block, block, pair.at[0, k], pair.at[1, k], (d, y * 2 + (1 - c))))
 
-    def gather_end(ref, buffer, sem, pair):
-        for k in range(n_y):
+    def gather_end(ref, buffer, sem, pair, which=None):
+        for k in which or range(n_y):
             source = lax.rem(y + n_y - k, n_y) * 2 + (1 - c)
             remote(ref, buffer.at[source], pair.at[0, k], pair.at[1, k], (d, source)).wait_recv()
 
@@ -180,8 +187,8 @@
         lax.broadcasted_iota(jnp.int32, (tok, tok), 0)
         < lax.broadcasted_iota(jnp.int32, (tok, tok), 1)
     ).astype(BF16)
-    codes, gates = [], []
-    for p in range(n_ex):
+
+    def codes_of(p, first):
         table, gate_table = routes[p].astype(F32), gate_tables[p]
         named = jnp.zeros((2 * local, tok), F32)
         gate = jnp.zeros((2 * local, tok), F32)
@@ -190,18 +197,137 @@
             named = jnp.where(hit, 1.0, named)
             gate = jnp.where(hit, gate_table[k : k + 1, :], gate)
         rank = jnp.dot(named.astype(BF16), before, preferred_element_type=F32)
-        codes.append(jnp.where(named > 0, rank + float(p * cap), -1.0))
-        gates.append(gate)
-    code = jnp.concatenate(codes, axis=1)
-    gate = jnp.concatenate(gates, axis=1)
-    row = lax.broadcasted_iota(jnp.int32, (slot_rows, tokens), 0).astype(F32)
-
-    def build(s, tokens_in):
+        return jnp.where(named > 0, rank + float(first), -1.0), gate
+
+    def joined(groups):
+        pairs = [codes_of(p, i * cap) for i, p in enumerate(groups)]
+        return [jnp.concatenate(parts, axis=1) for parts in zip(*pairs)]
+
+    def build(s, codes, tokens_in, height):
+        code, gate = codes
+        row = lax.broadcasted_iota(jnp.int32, (height, code.shape[1]), 0).astype(F32)
         hit = code[s : s + 1, :] == row
         scale = jnp.sum(jnp.where(hit, gate[s : s + 1, :], 0.0), axis=1, keepdims=True)
         chosen_rows = jnp.dot(hit.astype(BF16), tokens_in, preferred_element_type=F32)
         return (chosen_rows * scale).astype(BF16)
 
+    def pair_send(k, source, target):
+        send(
+            remote(
+                source.at[1 - x], target, pair_sem.at[0, k], pair_sem.at[1, k], (z * 2 + (1 - x), g)
+            )
+        )
+
+    zp, line = lax.rem(z, near), z // near
+    n_line = n_z // near
+
+    def near_start(u):
+        remote(
+            part.at[u, x], part_in.at[u], pair_sem.at[0, u], pair_sem.at[1, u], (z * 2 + (1 - x), g)
+        ).wait_recv()
+        pair_sum[u] = (part[u, x].astype(F32) + part_in[u].astype(F32)).astype(BF16)
+        if near == 2:
+            send(
+                remote(
+                    pair_sum.at[u, 1 - zp],
+                    near_in.at[u],
+                    near_sem.at[0, u],
+                    near_sem.at[1, u],
+                    ((line * 2 + (1 - zp)) * 2 + x, g),
+                )
+            )
+
+    def finished_line(u, i):
+        return lax.rem(y + n_y - u // CHUNKS, n_y) * steps + i
+
+    def far_copy(u, i):
+        to = finished_line(u, i)
+        apart = lax.rem(to + n_line - line, n_line)
+        return remote(
+            near_sum.at[u, 0, i],
+            far_in.at[u % CHUNKS, apart - 1],
+            far_sem.at[0, u, i],
+            far_sem.at[1, u % CHUNKS, apart],
+            ((to * near + zp) * 2 + x, g),
+        )
+
+    def far_start(u):
+        if near == 2:
+            remote(
+                pair_sum.at[u, zp],
+                near_in.at[u],
+                near_sem.at[0, u],
+                near_sem.at[1, u],
+                ((line * 2 + (1 - zp)) * 2 + x, g),
+            ).wait_recv()
+            near_sum[u, 0] = (pair_sum[u, zp].astype(F32) + near_in[u].astype(F32)).astype(BF16)
+        else:
+            near_sum[u, 0] = pair_sum[u, 0]
+        for i in range(steps):
+
+            @pl.when(finished_line(u, i) != line)
+            def _():
+                far_copy(u, i).start()
+
+    def spread_copy(k, j):
+        return remote(
+            total.at[k],
+            gathered.at[k, g],
+            spread_sem.at[0, k, j],
+            spread_sem.at[1, k, j],
+            (d, lax.rem(g + j, n_ex)),
+        )
+
+    def finish(u):
+        k = u % CHUNKS
+        for i in range(steps):
+
+            @pl.when(finished_line(u, i) == line)
+            def _():
+                result = near_sum[u, 0, i].astype(F32)
+                for apart in range(1, n_line):
+                    source = lax.rem(line + n_line - apart, n_line)
+                    remote(
+                        near_sum.at[u, 0, i],
+                        far_in.at[k, apart - 1],
+                        far_sem.at[0, u, i],
+                        far_sem.at[1, k, apart],
+                        ((source * near + zp) * 2 + x, g),
+                    ).wait_recv()
+                    result = result + far_in[k, apart - 1].astype(F32)
+                total[k] = result.astype(BF16)
+                gathered[k, g] = total[k]
+                for j in range(1, n_ex):
+                    spread_copy(k, j).start()
+
+    def multiply(o):
+        first = lax.rem(y + n_y - o, n_y) * 2
+        codes = joined([first, first + 1])
+        tokens_in = grads[pl.ds(first, 2)].reshape(2 * tok, columns)
+        for s in range(local):
+            picked[s] = build(s, codes, tokens_in, part_rows)
+        for k in range(CHUNKS):
+            u = o * CHUNKS + k
+            if o == 0:
+                loads[k].wait()
+            for s in range(local):
+                product[...] = lax.dot_general(
+                    picked[s],
+                    weights[s, k * width : (k + 1) * width, :],
+                    (((1,), (1,)), ((), ())),
+                    preferred_element_type=F32,
+                )
+                for t in range(n_dp // n_y):
+                    stage[t, s * piece : (s + 1) * piece, :] = product[t * piece : (t + 1) * piece, :]
+            for t in range(n_dp // n_y):
+                part[u, t % 2, t // 2 % near, t // 2 // near] = stage[t].astype(BF16)
+            pair_send(u, part.at[u], part_in.at[u])
+            if u >= CHUNKS:
+                near_start(u - CHUNKS)
+
+    own[4].wait()
+    gather_end(grad_ref, grads, grad_sem, grad_pair_sem, range(1))
+    multiply(0)
     gather_forward(grad_ref, grads, grad_sem, grad_pair_sem)
     gather_start(shared_ref, shareds, shared_sem, shared_pair_sem)
     for k in range(1, n_ex):
@@ -211,38 +337,15 @@
                 hidden_piece(peer), hiddens.at[g], hidden_sem.at[0, k], hidden_sem.at[1, k], (d, peer)
             )
         )
-    gather_end(grad_ref, grads, grad_sem, grad_pair_sem)
-    own[4].wait()
+    for o in range(1, n_y):
+        gather_end(grad_ref, grads, grad_sem, grad_pair_sem, range(o, o + 1))
+        multiply(o)
     all_tokens = grads[...].reshape(tokens, columns)
-
-    for s in range(local):
-        picked[s] = build(s, all_tokens)
-
-    def pair_send(k, source, target):
-        send(
-            remote(
-                source.at[1 - x], target, pair_sem.at[0, k], pair_sem.at[1, k], (z * 2 + (1 - x), g)
-            )
-        )
-
-    for k in range(CHUNKS):
-        loads[k].wait()
-        for s in range(local):
-            product[...] = lax.dot_general(
-                picked[s],
-                weights[s, k * width : (k + 1) * width, :],
-                (((1,), (1,)), ((), ())),
-                preferred_element_type=F32,
-            )
-            for t in range(n_dp):
-                stage[t, s * piece : (s + 1) * piece, :] = product[t * piece : (t + 1) * piece, :]
-        for t in range(n_dp):
-            part[k, t % 2, t // 2] = stage[t].astype(BF16)
-        pair_send(k, part.at[k], part_in.at[k])
+    all_codes = joined(range(n_ex))
 
     gather_forward(shared_ref, shareds, shared_sem, shared_pair_sem)
     for s in range(local):
-        rows[s] = build(local + s, all_tokens)
+        rows[s] = build(local + s, all_codes, all_tokens, slot_rows)
     gather_end(shared_ref, shareds, shared_sem, shared_pair_sem)
     own[5].wait()
     units = shared_ref.shape[0] * n_ex
@@ -256,7 +359,7 @@
             (((1,), (1,)), ((), ())),
             preferred_element_type=F32,
         ).astype(BF16)
-    pair_send(CHUNKS, spart, spart_in)
+    pair_send(units_sent, spart, spart_in)
 
     def ring_start(k, own, arrived, sums, landing):
         remote(
@@ -269,21 +372,21 @@
                 remote(
                     sums.at[to],
                     landing.at[step - 1],
-                    ring_sem.at[0, k, step],
-                    ring_sem.at[1, k, step],
+                    ring_sem.at[0, step],
+                    ring_sem.at[1, step],
                     (to * 2 + x, g),
                 )
             )
 
-    def ring_end(k, sums, landing):
+    def ring_end(sums, landing):
         result = sums[z].astype(F32)
         for step in range(1, n_z):
             source = lax.rem(z + n_z - step, n_z)
             remote(
                 sums.at[z],
                 landing.at[step - 1],
-                ring_sem.at[0, k, step],
-                ring_sem.at[1, k, step],
+                ring_sem.at[0, step],
+                ring_sem.at[1, step],
                 (source * 2 + x, g),
             ).wait_recv()
             result = result + landing[step - 1].astype(F32)
@@ -300,44 +403,39 @@
         stores.append(pltpu.make_async_copy(expert_grad.at[s], expert_grad_hbm.at[s], out_sem.at[s]))
         stores[-1].start()
 
-    for k in range(CHUNKS):
-        if k < local:
-            expert_weight_grad(k)
-        ring_start(k, part.at[k], part_in.at[k], pair_sum.at[k], ring_in.at[k])
-        if k == 1:
-            for j in range(1, n_ex):
-                source = lax.rem(g + n_ex - j, n_ex)
-                remote(
-                    hidden_piece(source),
-                    hiddens.at[source],
-                    hidden_sem.at[0, j],
-                    hidden_sem.at[1, j],
-                    (d, source),
-                ).wait_recv()
-            weight_grad_ref[...] = lax.dot_general(
-                hiddens[...].reshape(tokens, unit),
-                all_tokens,
-                (((0,), (0,)), ((), ())),
-                preferred_element_type=F32,
-            ).astype(BF16)
-    for s in range(CHUNKS, local):
+    early, late = range(units_sent - CHUNKS), range(units_sent - CHUNKS, units_sent)
+    for u in early:
+        far_start(u)
+    expert_weight_grad(0)
+    for u in late:
+        near_start(u)
+    for s in range(1, local // 2):
         expert_weight_grad(s)
-    ring_start(CHUNKS, spart, spart_in, spair_sum, sring_in)
-
-    for k in range(CHUNKS):
-        total[k] = ring_end(k, pair_sum.at[k], ring_in.at[k])
-        gathered[k, g] = total[k]
-        for j in range(1, n_ex):
-            send(
-                remote(
-                    total.at[k],
-                    gathered.at[k, g],
-                    spread_sem.at[0, k, j],
-                    spread_sem.at[1, k, j],
-                    (d, lax.rem(g + j, n_ex)),
-                )
-            )
-    hidden_grad_ref[...] = ring_end(CHUNKS, spair_sum, sring_in)
+    for u in early:
+        finish(u)
+    for u in late:
+        far_start(u)
+    for s in range(max(1, local // 2), local):
+        expert_weight_grad(s)
+    ring_start(units_sent, spart, spart_in, spair_sum, sring_in)
+    for u in late:
+        finish(u)
+    for j in range(1, n_ex):
+        source = lax.rem(g + n_ex - j, n_ex)
+        remote(
+            hidden_piece(source),
+            hiddens.at[source],
+            hidden_sem.at[0, j],
+            hidden_sem.at[1, j],
+            (d, source),
+        ).wait_recv()
+    weight_grad_ref[...] = lax.dot_general(
+        hiddens[...].reshape(tokens, unit),
+        all_tokens,
+        (((0,), (0,)), ((), ())),
+        preferred_element_type=F32,
+    ).astype(BF16)
+    hidden_grad_ref[...] = ring_end(spair_sum, sring_in)
 
     high = lax.broadcasted_iota(jnp.int32, (piece, local * piece), 0)
     wide = lax.broadcasted_iota(jnp.int32, (piece, local * piece), 1)
@@ -368,6 +466,15 @@
         copy.wait()
     for copy in sent:
         copy.wait_send()
+    for k in range(CHUNKS):
+        for j in range(1, n_ex):
+            spread_copy(k, j).wait_send()
+    for u in range(units_sent):
+        for i in range(steps):
+
+            @pl.when(finished_line(u, i) != line)
+            def _():
+                far_copy(u, i).wait_send()
 
 
 def on_device(
@@ -396,6 +503,10 @@
     width = hidden // CHUNKS
     share = units // n_dp
     n_z, n_y = n_dp // 2, n_ex // 2
+    ends = n_dp // n_y // 2
+    near = 2 if ends % 2 == 0 else 1
+    steps = ends // near
+    units_sent = n_y * CHUNKS
     vmem = pl.BlockSpec(memory_space=pltpu.VMEM)
     anywhere = pl.BlockSpec(memory_space=pl.ANY)
     sem = pltpu.SemaphoreType.DMA
@@ -421,13 +532,15 @@
             pltpu.VMEM((n_ex, chosen, tok), F32),
             pltpu.VMEM((n_ex, tok, units_here), BF16),
             pltpu.VMEM((n_ex, units_here, columns), BF16),
-            pltpu.VMEM((local, slot_rows, columns), BF16),
-            pltpu.VMEM((slot_rows, width), F32),
-            pltpu.VMEM((n_dp, packed, width), F32),
-            pltpu.VMEM((CHUNKS, 2, n_z, packed, width), BF16),
-            pltpu.VMEM((CHUNKS, n_z, packed, width), BF16),
-            pltpu.VMEM((CHUNKS, n_z, packed, width), BF16),
-            pltpu.VMEM((CHUNKS, n_z - 1, packed, width), BF16),
+            pltpu.VMEM((local, slot_rows // n_y, columns), BF16),
+            pltpu.VMEM((slot_rows // n_y, width), F32),
+            pltpu.VMEM((n_dp // n_y, packed, width), F32),
+            pltpu.VMEM((units_sent, 2, near, steps, packed, width), BF16),
+            pltpu.VMEM((units_sent, near, steps, packed, width), BF16),
+            pltpu.VMEM((units_sent, near, steps, packed, width), BF16),
+            pltpu.VMEM((units_sent, steps, packed, width), BF16),
+            pltpu.VMEM((units_sent, 1, steps, packed, width), BF16),
+            pltpu.VMEM((CHUNKS, n_z // near - 1, packed, width), BF16),
             pltpu.VMEM((CHUNKS, packed, width), BF16),
             pltpu.VMEM((CHUNKS, n_ex, packed, width), BF16),
             pltpu.VMEM((2, n_z, tok, share), BF16),
@@ -444,8 +557,10 @@
             sem((2, n_y)),
             sem((2, n_y)),
             sem((2, n_ex)),
-            sem((2, CHUNKS + 1)),
-            sem((2, CHUNKS + 1, n_z)),
+            sem((2, units_sent + 1)),
+            sem((2, units_sent)),
+            sem((2, units_sent, max(steps, n_z // near))),
+            sem((2, n_z)),
             sem((2, CHUNKS, n_ex)),
         ],
         compiler_params=pltpu.CompilerParams(

time: 56.8 us -> 58.5 us (1.030)
  Pallas kernels: 47 us -> 48.4 us
    pallas_call x1, Pallas kernels: 47 us -> 48.4 us  [on_device(): pl.pallas_call(functools.partial(exchange_kernel, n_dp, n_ex, sliced), ou...]
where the time goes in v1:
time: 58.5 us; the launch traced here: 58 us
  Pallas kernels  48.4 us (83%)
  local copies, waits for them, and re-layouts  9.03 us (15%)
  between operations  0.65 us (1%)
    pallas_call x1, Pallas kernels, on_device(): pl.pallas_call(functools.partial(exchange_kernel, n_dp, n_ex, sliced), ou...  48.4 us
    unnamed x7, local copies, waits for them, and re-layouts  7.31 us
    pallas_call x1, local copies, waits for them, and re-layouts, on_device(): pl.pallas_call(functools.partial(exchange_kernel, n_dp, n_ex, sliced), ou...  1.72 us

profile of v1, /device:TPU:0, one launch (start us, length us, event | category | flops | bytes accessed | tf_op | source)
XLA Modules:
  0.0 58.0 jit_solution(5852087746020242655)
XLA Ops:
  0.6 48.4 %shard_map.120 = (bf16[4,1024,768]{2,1,0:T(8,128)(2,1)}, bf16[4,20,1024]{2,1,0:T(8,128)(2,1)}, bf16[128,128]{1,0:T(8,128)(2,1)}, bf16[256,768]{1,0:T(8,128)(2,1)}) custom-call(bf16[128,768]{1,0:T(8,128)(2,1)} %grad_ref.1, s32[4,128]{1,0:T(4,128)} %bitcast.2, f32[4,128]{1,0:T(4,128)} %bitcast.3, s32[16]{0:T(128)} %old_hbm.1, s32[16]{0:T(128)} %new_hbm.1, ...), custom_call_target="tpu_custom_call" | custom-call | tf_op jit(solution)/shard_map/pallas_call | solution.py:513
  49.0 1.7 %copy.13 = bf16[4,20,1024]{2,0,1:T(4,128)(2,1)} copy(bf16[4,20,1024]{2,1,0:T(8,128)(2,1)} %get-tuple-element.5) | data formatting | bytes 327680 | tf_op jit(solution)/shard_map/pallas_call | solution.py:513
  50.7 0.0 copy-start.1
  50.7 0.0 copy-start
  50.7 5.9 %copy.17 = bf16[4,1024,768]{2,1,0:T(8,128)(2,1)} copy(bf16[4,1024,768]{2,1,0:T(8,128)(2,1)} %get-tuple-element.12) | data formatting | bytes 12582912
  56.7 0.0 copy-done.1
  56.7 0.6 %copy.18 = bf16[128,128]{1,0:T(8,128)(2,1)} copy(bf16[128,128]{1,0:T(8,128)(2,1)S(1)} %copy-done.1) | data formatting | bytes 65536
  57.3 0.0 copy-done
  57.3 0.7 %copy.19 = bf16[256,768]{1,0:T(8,128)(2,1)} copy(bf16[256,768]{1,0:T(8,128)(2,1)S(1)} %copy-done) | data formatting | bytes 786432
Async XLA Ops:
  50.7 5.9 %copy-start.1 = (bf16[128,128]{1,0:T(8,128)(2,1)S(1)}, bf16[128,128]{1,0:T(8,128)(2,1)}, u32[]{:S(2)}) copy-start(bf16[128,128]{1,0:T(8,128)(2,1)} %get-tuple-element.14) | copy-start | bytes 98308
  50.7 6.6 %copy-start = (bf16[256,768]{1,0:T(8,128)(2,1)S(1)}, bf16[256,768]{1,0:T(8,128)(2,1)}, u32[]{:S(2)}) copy-start(bf16[256,768]{1,0:T(8,128)(2,1)} %get-tuple-element.15) | copy-start | bytes 1179652
